TPU v7x, 256 devices: a whole 4x4x8 slice. The times are simulated.
256 devices in a mesh: gx: 8 (over y, core), gy: 4 (over x), gz: 8 (over z).
Axes of the slice: x: 4, y: 4, z: 8, core: 2. Of those that a mesh axis runs over, the one named last changes fastest.
Arguments:
- positions: float32 [8, 4, 8, 128, 3], P('gx', 'gy', 'gz'), may hold values from 0 to 1
- species: int32 [8, 4, 8, 128], P('gx', 'gy', 'gz'), may hold values from 0 to 4
- send_list: int32 [8, 4, 8, 27, 8], P('gx', 'gy', 'gz'), may hold values from -1 to 127, as said below
- pair_first: int32 [8, 4, 8, 2048], P('gx', 'gy', 'gz'), may hold values from 0 to 127, as said below
- pair_second: int32 [8, 4, 8, 2048], P('gx', 'gy', 'gz'), may hold values from -1 to 337, as said below
- species_embed: float32 [5, 64], replicated, may hold values from -6 to 6
- w_latent: bfloat16 [136, 256], replicated, may hold values from -2 to 2
- w_channel: bfloat16 [256, 192], replicated, may hold values from -0.375 to 0.375
- w_energy: bfloat16 [256, 128], replicated, may hold values from -0.375 to 0.375
- w_invariant: bfloat16 [192, 128], replicated, may hold values from -0.4375 to 0.4375
- energy_vector: float32 [128], replicated, may hold values from -0.5 to 0.5
Outputs:
- forces: float32 [8, 4, 8, 128, 3], P('gx', 'gy', 'gz')
- energy: float32 [1], replicated
Inputs may be any that keep to these rules, and one draw needn't show every extreme that they name: `send_list`: row s = 9a + 3b + c of a device's list names distinct owned atoms whose copies go to the device at offset (a - 1, b - 1, c - 1); used entries come first, -1 fills the rest; row 13 is all -1; every row other than 13 uses at least one entry; every device has a full row (8 entries) in every draw. `pair_first`: an owned atom; 0 where pair_second is -1. `pair_second`: -1 marks padding and follows all used entries of a device. A used entry is an owned atom other than the pair's first one, or the row 128 + s * 8 + k of block s whose column k the sending device fills. Some device uses all 2048 entries in every draw, and some entry reaches the largest value in every draw.
All inputs are finite; a program needn't handle non-finite values.
Results may differ from a plain program's by a relative error of at most 0.012.
The roundings to bfloat16 on the way count: a program that leaves them out, or rounds other values in their place, can miss the bound.
Values sent between devices are 32-bit elements; how exact they have to be, the bound alone decides.
No kernel may reach another device: no remote copies, remote signals or barrier semaphores. Data moves between devices by JAX's collectives and lax.ppermute only.
A program may use at most 64 MiB of HBM per device.

v0:
```python
import math

import jax
import jax.numpy as jnp
import numpy as np
from jax import lax
from jax.sharding import PartitionSpec as P

BLOCK = 256


DEGREE = np.array([0, 1, 1, 1, 2, 2, 2, 2, 2])
PARITY = np.array([1.0, -1.0, -1.0, -1.0, 1.0, 1.0, 1.0, 1.0, 1.0], dtype=np.float32)
ENV_SCALE = 0.1
RADIAL_STEP = 0.5
RADIAL_WIDTH = 0.35
ROOT_THREE = math.sqrt(3.0)
ROOT_FIVE = math.sqrt(5.0)
ROOT_FIFTEEN = math.sqrt(15.0)


def extended(cells, sides, width):
    for axis, dim in sides:
        count = lax.axis_size(axis)
        head = lax.slice_in_dim(cells, 0, width, axis=dim)
        tail = lax.slice_in_dim(cells, cells.shape[dim] - width, cells.shape[dim], axis=dim)
        cells = jnp.concatenate(
            [
                lax.ppermute(tail, axis, [(i, (i + 1) % count) for i in range(count)]),
                cells,
                lax.ppermute(head, axis, [((i + 1) % count, i) for i in range(count)]),
            ],
            axis=dim,
        )
    return cells


def harmonics(displace):
    coord_x = displace[:, 0]
    coord_y = displace[:, 1]
    coord_z = displace[:, 2]
    radius_sq = coord_x * coord_x + coord_y * coord_y + coord_z * coord_z
    return jnp.stack(
        [
            jnp.ones_like(coord_x),
            ROOT_THREE * coord_x,
            ROOT_THREE * coord_y,
            ROOT_THREE * coord_z,
            ROOT_FIFTEEN * coord_x * coord_y,
            ROOT_FIFTEEN * coord_y * coord_z,
            0.5 * ROOT_FIVE * (3.0 * coord_z * coord_z - radius_sq),
            ROOT_FIFTEEN * coord_x * coord_z,
            0.5 * ROOT_FIFTEEN * (coord_x * coord_x - coord_y * coord_y),
        ],
        axis=1,
    )


def pair_latent(displace, onehot_first, onehot_second, species_embed, w_latent, w_channel):
    radius_sq = jnp.sum(displace * displace, axis=1)
    basis_count = w_latent.shape[0] - 2 * species_embed.shape[1]
    centres = RADIAL_STEP * jnp.arange(basis_count).astype(displace.dtype)
    radial = jnp.exp(-jnp.square((radius_sq[:, None] - centres[None, :]) / RADIAL_WIDTH))
    embed_first = jnp.dot(onehot_first, species_embed, precision=lax.Precision.HIGHEST)
    embed_second = jnp.dot(onehot_second, species_embed, precision=lax.Precision.HIGHEST)
    features = jnp.concatenate(
        [radial, embed_first + embed_second, embed_first * embed_second], axis=1
    ).astype(jnp.bfloat16)
    hidden = jax.nn.silu(jnp.dot(features, w_latent, preferred_element_type=jnp.float32))
    hidden_low = hidden.astype(jnp.bfloat16)
    weights = (
        jnp.dot(hidden_low, w_channel, preferred_element_type=jnp.float32)
        * jnp.exp(-0.5 * radius_sq)[:, None]
    )
    return (hidden_low, weights)


def pair_tensors(displace, weights):
    row_count = weights.shape[0]
    channels = weights.shape[1] // 3
    solid = harmonics(displace)
    per_component = weights.reshape(row_count, 3, channels)[:, DEGREE, :]
    tensor_first = (per_component * solid[:, :, None]).reshape(row_count, 9 * channels)
    tensor_second = (per_component * (solid * PARITY)[:, :, None]).reshape(row_count, 9 * channels)
    return (tensor_first, tensor_second)


def pair_env(displace, onehot_first, onehot_second, valid_mask, species_embed, w_latent, w_channel):
    hidden_low, weights = pair_latent(
        displace, onehot_first, onehot_second, species_embed, w_latent, w_channel
    )
    tensor_first, tensor_second = pair_tensors(displace, weights)
    pair_scale = ENV_SCALE * valid_mask[:, None]
    return (pair_scale * tensor_first, pair_scale * tensor_second)


def invariants(tensor, environ):
    row_count = tensor.shape[0]
    channels = tensor.shape[1] // 9
    product = (tensor * environ).reshape(row_count, 9, channels)
    return jnp.concatenate(
        [product[:, 0], jnp.sum(product[:, 1:4], axis=1), jnp.sum(product[:, 4:9], axis=1)], axis=1
    )


def pair_energy(
    displace,
    onehot_first,
    onehot_second,
    env_first,
    env_second,
    valid_mask,
    species_embed,
    w_latent,
    w_channel,
    w_energy,
    w_invariant,
    energy_vector,
):
    hidden_low, weights = pair_latent(
        displace, onehot_first, onehot_second, species_embed, w_latent, w_channel
    )
    tensor_first, tensor_second = pair_tensors(displace, weights)
    shared = jnp.dot(hidden_low, w_energy, preferred_element_type=jnp.float32)

    def centre(tensor, environ):
        inv_low = invariants(tensor, environ).astype(jnp.bfloat16)
        active = jax.nn.silu(
            shared + jnp.dot(inv_low, w_invariant, preferred_element_type=jnp.float32)
        )
        return jnp.dot(active, energy_vector, precision=lax.Precision.HIGHEST)

    return jnp.sum(
        valid_mask * (centre(tensor_first, env_first) + centre(tensor_second, env_second))
    )


def trade(outgoing):
    padded = extended(outgoing, (("gx", 0), ("gy", 1), ("gz", 2)), 1)
    return padded[::2, ::2, ::2]


def per_device(
    positions,
    species,
    send_list,
    pair_first,
    pair_second,
    species_embed,
    w_latent,
    w_channel,
    w_energy,
    w_invariant,
    energy_vector,
):
    own_pos = positions.reshape(-1, 3)
    atom_count = own_pos.shape[0]
    sends = send_list.reshape(27, -1)
    ghost_slots = sends.shape[1]
    ghost_total = 27 * ghost_slots
    row_total = atom_count + ghost_total
    width = 9 * species_embed.shape[1]
    present = (sends >= 0).reshape(-1, 1).astype(jnp.float32)
    send_rows = jnp.maximum(sends, 0).reshape(-1)
    return_rows = jnp.where(sends >= 0, sends, atom_count).reshape(-1)
    slot_offsets = np.array(
        [
            [slot_index // 9 - 1, slot_index // 3 % 3 - 1, slot_index % 3 - 1]
            for slot_index in range(27)
        ],
        dtype=np.float32,
    )
    ghost_shift = jnp.asarray(np.repeat(slot_offsets, ghost_slots, axis=0))

    def forward(own_rows):
        columns = own_rows.shape[1]
        outgoing = (jnp.take(own_rows, send_rows, axis=0) * present).reshape(
            3, 3, 3, ghost_slots, columns
        )
        return trade(outgoing).reshape(ghost_total, columns)

    def backward(table_rows):
        columns = table_rows.shape[1]
        incoming = trade(table_rows[atom_count:].reshape(3, 3, 3, ghost_slots, columns))
        return (
            table_rows[:atom_count]
            .at[return_rows]
            .add(incoming.reshape(ghost_total, columns), mode="drop")
        )

    own_onehot = jax.nn.one_hot(species.reshape(-1), species_embed.shape[0], dtype=jnp.float32)
    ghost_data = forward(jnp.concatenate([own_pos, own_onehot], axis=1))
    table_pos = jnp.concatenate([own_pos, ghost_data[:, :3] + ghost_shift], axis=0)
    table_onehot = jnp.concatenate([own_onehot, ghost_data[:, 3:]], axis=0)
    firsts_all = pair_first.reshape(-1)
    seconds_all = pair_second.reshape(-1)
    used_blocks = (jnp.sum((seconds_all >= 0).astype(jnp.int32)) + BLOCK - 1) // BLOCK

    def block_pairs(block_index):
        offset_rows = block_index * BLOCK
        first_rows = lax.dynamic_slice_in_dim(firsts_all, offset_rows, BLOCK)
        second_raw = lax.dynamic_slice_in_dim(seconds_all, offset_rows, BLOCK)
        valid_mask = (second_raw >= 0).astype(jnp.float32)
        second_rows = jnp.maximum(second_raw, 0)
        displace = table_pos[second_rows] - table_pos[first_rows]
        return (first_rows, second_rows, valid_mask, displace)

    def env_block(block_index, env_part):
        first_rows, second_rows, valid_mask, displace = block_pairs(block_index)
        part_first, part_second = pair_env(
            displace,
            table_onehot[first_rows],
            table_onehot[second_rows],
            valid_mask,
            species_embed,
            w_latent,
            w_channel,
        )
        return env_part.at[first_rows].add(part_first).at[second_rows].add(part_second)

    env_part = lax.fori_loop(0, used_blocks, env_block, jnp.zeros((row_total, width), jnp.float32))
    env_own = backward(env_part)
    table_env = jnp.concatenate([env_own, forward(env_own)], axis=0)

    def energy_block(block_index, totals):
        energy_sum, grad_pos, grad_env = totals
        first_rows, second_rows, valid_mask, displace = block_pairs(block_index)
        onehot_first = table_onehot[first_rows]
        onehot_second = table_onehot[second_rows]

        def block_energy(displace_in, env_first, env_second):
            return pair_energy(
                displace_in,
                onehot_first,
                onehot_second,
                env_first,
                env_second,
                valid_mask,
                species_embed,
                w_latent,
                w_channel,
                w_energy,
                w_invariant,
                energy_vector,
            )

        energy_part, pullback = jax.vjp(
            block_energy, displace, table_env[first_rows], table_env[second_rows]
        )
        grad_disp, grad_first, grad_second = pullback(jnp.ones_like(energy_part))
        grad_pos = grad_pos.at[first_rows].add(-grad_disp).at[second_rows].add(grad_disp)
        grad_env = grad_env.at[first_rows].add(grad_first).at[second_rows].add(grad_second)
        return (energy_sum + energy_part, grad_pos, grad_env)

    start_totals = (
        jnp.zeros((), jnp.float32),
        jnp.zeros((row_total, 3), jnp.float32),
        jnp.zeros((row_total, width), jnp.float32),
    )
    energy_sum, grad_pos, grad_env = lax.fori_loop(0, used_blocks, energy_block, start_totals)
    adjoint_own = backward(grad_env)
    table_adjoint = jnp.concatenate([adjoint_own, forward(adjoint_own)], axis=0)

    def force_block(block_index, grad_pos):
        first_rows, second_rows, valid_mask, displace = block_pairs(block_index)
        onehot_first = table_onehot[first_rows]
        onehot_second = table_onehot[second_rows]

        def block_env(displace_in):
            return pair_env(
                displace_in,
                onehot_first,
                onehot_second,
                valid_mask,
                species_embed,
                w_latent,
                w_channel,
            )

        unused_env, pullback = jax.vjp(block_env, displace)
        (grad_disp,) = pullback((table_adjoint[first_rows], table_adjoint[second_rows]))
        return grad_pos.at[first_rows].add(-grad_disp).at[second_rows].add(grad_disp)

    grad_pos = lax.fori_loop(0, used_blocks, force_block, grad_pos)
    forces = -backward(grad_pos)
    grand_total = lax.psum(energy_sum, ("gx", "gy", "gz"))
    atoms_all = atom_count * lax.axis_size("gx") * lax.axis_size("gy") * lax.axis_size("gz")
    return (forces.reshape(positions.shape), (grand_total / atoms_all).reshape(1))


def solution(mesh):
    return jax.shard_map(
        per_device,
        mesh=mesh,
        in_specs=(
            P("gx", "gy", "gz", None, None),
            P("gx", "gy", "gz", None),
            P("gx", "gy", "gz", None, None),
            P("gx", "gy", "gz", None),
            P("gx", "gy", "gz", None),
            P(),
            P(),
            P(),
            P(),
            P(),
            P(),
        ),
        out_specs=(P("gx", "gy", "gz", None, None), P()),
        check_vma=False,
    )
```

profile of v0, /device:TPU:1, one launch (start us, length us, event | category | flops | bytes accessed | tf_op | source)
XLA Modules:
  0.0 992.1 jit_solution(15634093773546428148)
XLA Ops:
  18.9 5.7 collective-permute-start.5
  32.8 80.1 %while.41 = (s32[]{:T(128)}, f32[344,576]{1,0:T(8,128)S(1)}, s32[]{:T(128)}, s32[2048]{0:T(1024)}, s32[2048]{0:T(1024)}, /*index=5*/f32[344,3]{1,0:T(8,128)S(1)}...) while((s32[]{:T(128)}, f32[344,576]{1,0:T(8,128)S(1)}, ...), condition=%wide.region_5.6_spmd.clone, body=%wide.region_1.5_spmd.sunk.clone.sunk | while | flops 46518036 | bytes 12009355 | solution.py:221
  113.0 4.4 collective-permute-start.6
  120.6 11.2 %collective-permute-done.6 = f32[1,3,3,8,576]{4,3,2,1,0:T(8,128)S(1)} collective-permute-done((f32[1,3,3,8,576]{4,3,2,1,0:T(8,128)S(1)}, f32[1,3,3,8,576]{4,3,2,1,0:T(8,128)S(1)}, u32[]{:S(2)}, u32[]{:S(2)}) %collective-permute-start.6) | collective-permute-done | bytes 165920 | tf_op jit(solution)/shard_map/ppermute | solution.py:29
  131.8 12.9 %collective-permute-start.9 = (f32[5,1,3,8,576]{4,3,2,1,0:T(8,128)S(1)}, f32[5,1,3,8,576]{4,3,2,1,0:T(8,128)S(1)}, u32[]{:S(2)}, u32[]{:S(2)}) collective-permute-start(f32[5,1,3,8,576]{4,3,2,1,0:T(8,128)S(1)} %get-tuple-element.911), channel_id=1, source_target_pairs={{8,0},{16,8},{24,16},{0,24},{9,1},{17,9},{25,17},{1,25},{10,2},{18... | collective-permute-start | bytes 829448 | tf_op jit(solution)/shard_map/ppermute | solution.py:31
  151.7 4.3 collective-permute-start.11
  156.0 12.3 %collective-permute-start.10 = (f32[5,5,1,8,576]{4,3,2,1,0:T(8,128)S(1)}, f32[5,5,1,8,576]{4,3,2,1,0:T(8,128)S(1)}, u32[]{:S(2)}, u32[]{:S(2)}) collective-permute-start(f32[5,5,1,8,576]{4,3,2,1,0:T(8,128)S(1)} %get-tuple-element.902), channel_id=1, source_target_pairs={{0,1},{1,2},{2,3},{3,4},{4,5},{5,6},{6,7},{7,0},{8,9},{9,10},{10,1... | collective-permute-start | bytes 1382408 | tf_op jit(solution)/shard_map/ppermute | solution.py:29
  168.4 9.0 collective-permute-done.10
  181.0 6.3 collective-permute-start.13
  202.9 6.6 collective-permute-done.17
  212.9 331.1 %while.42 = (s32[]{:T(128)}, f32[]{:T(128)}, f32[344,3]{1,0:T(8,128)S(1)}, f32[344,576]{1,0:T(8,128)S(1)}, s32[]{:T(128)}, /*index=5*/s32[2048]{0:T(1024)}, f32[...) while((s32[]{:T(128)}, f32[]{:T(128)}, ...), condition=%wide.region_23.25_spmd.clone, body=%wide.region_7.24_spmd.sunk.clone.sunk | while | flops 181073168 | bytes 50737132 | solution.py:260
  544.1 10.7 %collective-permute-start.18 = (f32[1,3,3,8,576]{4,3,2,1,0:T(8,128)S(1)}, f32[1,3,3,8,576]{4,3,2,1,0:T(8,128)S(1)}, u32[]{:S(2)}, u32[]{:S(2)}) collective-permute-start(f32[1,3,3,8,576]{4,3,2,1,0:T(8,128)S(1)} %bitcast.285), channel_id=1, source_target_pairs={{0,32},{32,64},{64,96},{96,128},{128,160},{160,192},{192,224},{224... | collective-permute-start | bytes 497672 | tf_op jit(solution)/shard_map/ppermute | solution.py:29
  558.0 54.1 %collective-permute-done.18 = f32[1,3,3,8,576]{4,3,2,1,0:T(8,128)S(1)} collective-permute-done((f32[1,3,3,8,576]{4,3,2,1,0:T(8,128)S(1)}, f32[1,3,3,8,576]{4,3,2,1,0:T(8,128)S(1)}, u32[]{:S(2)}, u32[]{:S(2)}) %collective-permute-start.18) | collective-permute-done | bytes 165920 | tf_op jit(solution)/shard_map/ppermute | solution.py:29
  612.2 47.5 %collective-permute-start.21 = (f32[5,1,3,8,576]{4,3,2,1,0:T(8,128)S(1)}, f32[5,1,3,8,576]{4,3,2,1,0:T(8,128)S(1)}, u32[]{:S(2)}, u32[]{:S(2)}) collective-permute-start(f32[5,1,3,8,576]{4,3,2,1,0:T(8,128)S(1)} %get-tuple-element.907), channel_id=1, source_target_pairs={{8,0},{16,8},{24,16},{0,24},{9,1},{17,9},{25,17},{1,25},{10,2},{18... | collective-permute-start | bytes 829448 | tf_op jit(solution)/shard_map/ppermute | solution.py:31
  659.8 7.9 collective-permute-start.20
  675.5 6.3 collective-permute-done.23
  686.7 8.6 collective-permute-start.25
  711.5 6.6 collective-permute-done.29
  721.6 127.2 %while.43 = (s32[]{:T(128)}, f32[344,3]{1,0:T(8,128)S(1)}, s32[]{:T(128)}, s32[2048]{0:T(1024)}, s32[2048]{0:T(1024)}, /*index=5*/f32[344,3]{1,0:T(8,128)S(1)}, ...) while((s32[]{:T(128)}, f32[344,3]{1,0:T(8,128)S(1)}, ...), condition=%wide.region_34.36_spmd.clone, body=%wide.region_25.35_spmd.sunk.clone.sunk | while | flops 91058448 | bytes 15298459 | solution.py:284
  849.2 11.8 %collective-permute-start.30 = (f32[1,3,3,8,3]{3,2,1,4,0:T(4,128)S(1)}, f32[1,3,3,8,3]{3,2,1,4,0:T(4,128)S(1)}, u32[]{:S(2)}, u32[]{:S(2)}) collective-permute-start(f32[1,3,3,8,3]{3,2,1,4,0:T(4,128)S(1)} %copy.278), channel_id=1, source_target_pairs={{0,32},{32,64},{64,96},{96,128},{128,160},{160,192},{192,224},{224... | collective-permute-start | bytes 2600 | tf_op jit(solution)/shard_map/ppermute | solution.py:29
  862.3 19.6 %collective-permute-done.30 = f32[1,3,3,8,3]{3,2,1,4,0:T(4,128)S(1)} collective-permute-done((f32[1,3,3,8,3]{3,2,1,4,0:T(4,128)S(1)}, f32[1,3,3,8,3]{3,2,1,4,0:T(4,128)S(1)}, u32[]{:S(2)}, u32[]{:S(2)}) %collective-permute-start.30) | collective-permute-done | bytes 896 | tf_op jit(solution)/shard_map/ppermute | solution.py:29
  882.1 12.7 %collective-permute-start.33 = (f32[5,1,3,8,3]{4,3,2,1,0:T(8,128)S(1)}, f32[5,1,3,8,3]{4,3,2,1,0:T(8,128)S(1)}, u32[]{:S(2)}, u32[]{:S(2)}) collective-permute-start(f32[5,1,3,8,3]{4,3,2,1,0:T(8,128)S(1)} %get-tuple-element.927), channel_id=1, source_target_pairs={{8,0},{16,8},{24,16},{0,24},{9,1},{17,9},{25,17},{1,25},{10,2},{18... | collective-permute-start | bytes 4328 | tf_op jit(solution)/shard_map/ppermute | solution.py:31
  894.8 8.0 collective-permute-start.32
  908.5 79.1 %psum.7 = f32[]{:T(128)} all-reduce(f32[]{:T(128)} %get-tuple-element.1539), channel_id=1, replica_groups=mesh['gx'=8,'gy'=4,'gz'=8] {'gx','gy','gz'}, use_global_device_ids=true, to_apply=%region_36.38 | all-reduce | flops 1 | bytes 8 | tf_op jit(solution)/shard_map/psum | solution.py:286
  (1642 shorter events, 631.3 us)
Async XLA Ops:
  18.9 7.7 collective-permute-start.5
  112.9 7.7 collective-permute-start.7
  113.0 18.8 %collective-permute-start.6 = (f32[1,3,3,8,576]{4,3,2,1,0:T(8,128)S(1)}, f32[1,3,3,8,576]{4,3,2,1,0:T(8,128)S(1)}, u32[]{:S(2)}, u32[]{:S(2)}) collective-permute-start(f32[1,3,3,8,576]{4,3,2,1,0:T(8,128)S(1)} %bitcast.284), channel_id=1, source_target_pairs={{0,32},{32,64},{64,96},{96,128},{128,160},{160,192},{192,224},{224... | collective-permute-start | bytes 497672 | tf_op jit(solution)/shard_map/ppermute | solution.py:29
  131.8 18.6 %collective-permute-start.9 = (f32[5,1,3,8,576]{4,3,2,1,0:T(8,128)S(1)}, f32[5,1,3,8,576]{4,3,2,1,0:T(8,128)S(1)}, u32[]{:S(2)}, u32[]{:S(2)}) collective-permute-start(f32[5,1,3,8,576]{4,3,2,1,0:T(8,128)S(1)} %get-tuple-element.911), channel_id=1, source_target_pairs={{8,0},{16,8},{24,16},{0,24},{9,1},{17,9},{25,17},{1,25},{10,2},{18... | collective-permute-start | bytes 829448 | tf_op jit(solution)/shard_map/ppermute | solution.py:31
  151.7 16.7 %collective-permute-start.11 = (f32[5,5,1,8,576]{4,3,2,1,0:T(8,128)S(1)}, f32[5,5,1,8,576]{4,3,2,1,0:T(8,128)S(1)}, u32[]{:S(2)}, u32[]{:S(2)}) collective-permute-start(f32[5,5,1,8,576]{4,3,2,1,0:T(8,128)S(1)} %get-tuple-element.903), channel_id=1, source_target_pairs={{1,0},{2,1},{3,2},{4,3},{5,4},{6,5},{7,6},{0,7},{9,8},{10,9},{11,1... | collective-permute-start | bytes 1382408 | tf_op jit(solution)/shard_map/ppermute | solution.py:31
  156.0 21.4 %collective-permute-start.10 = (f32[5,5,1,8,576]{4,3,2,1,0:T(8,128)S(1)}, f32[5,5,1,8,576]{4,3,2,1,0:T(8,128)S(1)}, u32[]{:S(2)}, u32[]{:S(2)}) collective-permute-start(f32[5,5,1,8,576]{4,3,2,1,0:T(8,128)S(1)} %get-tuple-element.902), channel_id=1, source_target_pairs={{0,1},{1,2},{2,3},{3,4},{4,5},{5,6},{6,7},{7,0},{8,9},{9,10},{10,1... | collective-permute-start | bytes 1382408 | tf_op jit(solution)/shard_map/ppermute | solution.py:29
  181.0 8.7 collective-permute-start.13
  201.4 8.1 collective-permute-start.17
  201.4 9.4 collective-permute-start.16
  544.1 14.0 %collective-permute-start.19 = (f32[1,3,3,8,576]{4,3,2,1,0:T(8,128)S(1)}, f32[1,3,3,8,576]{4,3,2,1,0:T(8,128)S(1)}, u32[]{:S(2)}, u32[]{:S(2)}) collective-permute-start(f32[1,3,3,8,576]{4,3,2,1,0:T(8,128)S(1)} %bitcast.289), channel_id=1, source_target_pairs={{32,0},{64,32},{96,64},{128,96},{160,128},{192,160},{224,192},{0,2... | collective-permute-start | bytes 497672 | tf_op jit(solution)/shard_map/ppermute | solution.py:31
  544.1 68.1 %collective-permute-start.18 = (f32[1,3,3,8,576]{4,3,2,1,0:T(8,128)S(1)}, f32[1,3,3,8,576]{4,3,2,1,0:T(8,128)S(1)}, u32[]{:S(2)}, u32[]{:S(2)}) collective-permute-start(f32[1,3,3,8,576]{4,3,2,1,0:T(8,128)S(1)} %bitcast.285), channel_id=1, source_target_pairs={{0,32},{32,64},{64,96},{96,128},{128,160},{160,192},{192,224},{224... | collective-permute-start | bytes 497672 | tf_op jit(solution)/shard_map/ppermute | solution.py:29
  612.2 59.6 %collective-permute-start.21 = (f32[5,1,3,8,576]{4,3,2,1,0:T(8,128)S(1)}, f32[5,1,3,8,576]{4,3,2,1,0:T(8,128)S(1)}, u32[]{:S(2)}, u32[]{:S(2)}) collective-permute-start(f32[5,1,3,8,576]{4,3,2,1,0:T(8,128)S(1)} %get-tuple-element.907), channel_id=1, source_target_pairs={{8,0},{16,8},{24,16},{0,24},{9,1},{17,9},{25,17},{1,25},{10,2},{18... | collective-permute-start | bytes 829448 | tf_op jit(solution)/shard_map/ppermute | solution.py:31
  659.8 13.9 %collective-permute-start.20 = (f32[5,1,3,8,576]{4,3,2,1,0:T(8,128)S(1)}, f32[5,1,3,8,576]{4,3,2,1,0:T(8,128)S(1)}, u32[]{:S(2)}, u32[]{:S(2)}) collective-permute-start(f32[5,1,3,8,576]{4,3,2,1,0:T(8,128)S(1)} %get-tuple-element.906), channel_id=1, source_target_pairs={{0,8},{8,16},{16,24},{24,0},{1,9},{9,17},{17,25},{25,1},{2,10},{10... | collective-permute-start | bytes 829448 | tf_op jit(solution)/shard_map/ppermute | solution.py:29
  673.7 8.0 collective-permute-start.23
  673.8 9.2 collective-permute-start.22
  686.7 13.1 %collective-permute-start.25 = (f32[1,3,3,8,576]{4,3,2,1,0:T(8,128)S(1)}, f32[1,3,3,8,576]{4,3,2,1,0:T(8,128)S(1)}, u32[]{:S(2)}, u32[]{:S(2)}) collective-permute-start(f32[1,3,3,8,576]{4,3,2,1,0:T(8,128)S(1)} %bitcast.291), channel_id=1, source_target_pairs={{32,0},{64,32},{96,64},{128,96},{160,128},{192,160},{224,192},{0,2... | collective-permute-start | bytes 497672 | tf_op jit(solution)/shard_map/ppermute | solution.py:31
  710.0 8.1 collective-permute-start.29
  710.3 9.4 collective-permute-start.28
  849.0 13.2 %collective-permute-start.31 = (f32[1,3,3,8,3]{3,2,1,4,0:T(4,128)S(1)}, f32[1,3,3,8,3]{3,2,1,4,0:T(4,128)S(1)}, u32[]{:S(2)}, u32[]{:S(2)}) collective-permute-start(f32[1,3,3,8,3]{3,2,1,4,0:T(4,128)S(1)} %copy.279), channel_id=1, source_target_pairs={{32,0},{64,32},{96,64},{128,96},{160,128},{192,160},{224,192},{0,2... | collective-permute-start | bytes 2600 | tf_op jit(solution)/shard_map/ppermute | solution.py:31
  849.2 32.8 %collective-permute-start.30 = (f32[1,3,3,8,3]{3,2,1,4,0:T(4,128)S(1)}, f32[1,3,3,8,3]{3,2,1,4,0:T(4,128)S(1)}, u32[]{:S(2)}, u32[]{:S(2)}) collective-permute-start(f32[1,3,3,8,3]{3,2,1,4,0:T(4,128)S(1)} %copy.278), channel_id=1, source_target_pairs={{0,32},{32,64},{64,96},{96,128},{128,160},{160,192},{192,224},{224... | collective-permute-start | bytes 2600 | tf_op jit(solution)/shard_map/ppermute | solution.py:29
  882.1 22.3 %collective-permute-start.33 = (f32[5,1,3,8,3]{4,3,2,1,0:T(8,128)S(1)}, f32[5,1,3,8,3]{4,3,2,1,0:T(8,128)S(1)}, u32[]{:S(2)}, u32[]{:S(2)}) collective-permute-start(f32[5,1,3,8,3]{4,3,2,1,0:T(8,128)S(1)} %get-tuple-element.927), channel_id=1, source_target_pairs={{8,0},{16,8},{24,16},{0,24},{9,1},{17,9},{25,17},{1,25},{10,2},{18... | collective-permute-start | bytes 4328 | tf_op jit(solution)/shard_map/ppermute | solution.py:31
  894.8 10.5 %collective-permute-start.32 = (f32[5,1,3,8,3]{4,3,2,1,0:T(8,128)S(1)}, f32[5,1,3,8,3]{4,3,2,1,0:T(8,128)S(1)}, u32[]{:S(2)}, u32[]{:S(2)}) collective-permute-start(f32[5,1,3,8,3]{4,3,2,1,0:T(8,128)S(1)} %get-tuple-element.926), channel_id=1, source_target_pairs={{0,8},{8,16},{16,24},{24,0},{1,9},{9,17},{17,25},{25,1},{2,10},{10... | collective-permute-start | bytes 4328 | tf_op jit(solution)/shard_map/ppermute | solution.py:29
  905.4 82.9 %collective-permute-start.35 = (f32[5,5,1,8,3]{4,3,2,1,0:T(8,128)S(1)}, f32[5,5,1,8,3]{4,3,2,1,0:T(8,128)S(1)}, u32[]{:S(2)}, u32[]{:S(2)}) collective-permute-start(f32[5,5,1,8,3]{4,3,2,1,0:T(8,128)S(1)} %get-tuple-element.923), channel_id=1, source_target_pairs={{1,0},{2,1},{3,2},{4,3},{5,4},{6,5},{7,6},{0,7},{9,8},{10,9},{11,1... | collective-permute-start | bytes 7208 | tf_op jit(solution)/shard_map/ppermute | solution.py:31
  905.5 82.8 %collective-permute-start.34 = (f32[5,5,1,8,3]{4,3,2,1,0:T(8,128)S(1)}, f32[5,5,1,8,3]{4,3,2,1,0:T(8,128)S(1)}, u32[]{:S(2)}, u32[]{:S(2)}) collective-permute-start(f32[5,5,1,8,3]{4,3,2,1,0:T(8,128)S(1)} %get-tuple-element.922), channel_id=1, source_target_pairs={{0,1},{1,2},{2,3},{3,4},{4,5},{5,6},{6,7},{7,0},{8,9},{9,10},{10,1... | collective-permute-start | bytes 7208 | tf_op jit(solution)/shard_map/ppermute | solution.py:29
  (331 other events, 1465.6 us)
where the time goes:
time: 1000 us; the launch traced here: 992 us
  other arithmetic  283 us (28%)
  local copies, waits for them, and re-layouts  178 us (18%)
  starting transfers between devices  173 us (17%)
  waiting for transfers between devices  169 us (17%)
  matrix products  94.5 us (9%)
  blocking collectives  79.1 us (8%)
  loops' own time  11 us (1%)
    ppermute x18, waiting for transfers between devices, extended(): lax.ppermute(tail, axis, [(i, (i + 1) % count) for i in range(count)])  116 us
    ppermute x18, starting transfers between devices, extended(): lax.ppermute(head, axis, [((i + 1) % count, i) for i in range(count)])  106 us
    psum x1, blocking collectives, per_device(): grand_total = lax.psum(energy_sum, ('gx', 'gy', 'gz'))  79.1 us
    ppermute x18, starting transfers between devices, extended(): lax.ppermute(tail, axis, [(i, (i + 1) % count) for i in range(count)])  66.9 us
    ppermute x18, waiting for transfers between devices, extended(): lax.ppermute(head, axis, [((i + 1) % count, i) for i in range(count)])  52.9 us
    dot_general x24, matrix products, pair_latent(): jnp.dot(features, w_latent, preferred_element_type=jnp.float32)  34.2 us
    scatter-add x12, other arithmetic, energy_block(): grad_env.at[first_rows].add(grad_first).at[second_rows].add(grad_second)  31.7 us
    scatter-add x12, other arithmetic, env_block(): env_part.at[first_rows].add(part_first).at[second_rows].add(part_second)  30.9 us
  transfers between devices with their start and end apart: 36, of which 31 were waited for; matrix products, arithmetic and copies ran while one was open for 0% of the time, Pallas kernels for 0%

commit v1 on v0

--- a/solution.py
+++ b/solution.py
@@ -4,6 +4,9 @@
 import jax.numpy as jnp
 import numpy as np
 from jax import lax
+from jax.experimental import pallas as pl
+from jax.experimental.layout import Layout, with_layout_constraint
+from jax.experimental.pallas import tpu as pltpu
 from jax.sharding import PartitionSpec as P
 
 BLOCK = 256
@@ -140,7 +143,7 @@
     return padded[::2, ::2, ::2]
 
 
-def per_device(
+def general(
     positions,
     species,
     send_list,
@@ -288,6 +291,834 @@
     return (forces.reshape(positions.shape), (grand_total / atoms_all).reshape(1))
 
 
+PACK = 256
+PART = 3
+CHUNK = PART * 128
+ATOMS = 128
+SLOTS = 27
+GHOSTS = 8
+LANES = 128
+CAP = LANES - GHOSTS
+HERE = 13
+SIDE_ROWS = 9 * 8
+OWN_TILES = 16
+GROUPS = 32
+MASKED = 10
+C = 64
+WIDTH = 9 * C
+NB = 8
+NSPEC = 5
+COMBOS = 32
+OWN_CHUNKS = -(-OWN_TILES // PART)
+EDGE_CHUNKS = -(-42 // PART)
+CHUNKS = OWN_CHUNKS + EDGE_CHUNKS
+EDGE_START = OWN_CHUNKS * PART
+
+R3, R5, R15 = ROOT_THREE, ROOT_FIVE, ROOT_FIFTEEN
+
+LEVEL = (0, 2, 2, 2, 2, 2, 1, 1, 1)
+EVEN = 6 * C
+
+F32 = jnp.float32
+BF16 = jnp.bfloat16
+NN = (((1,), (0,)), ((), ()))
+NT = (((1,), (1,)), ((), ()))
+TN = (((0,), (0,)), ((), ()))
+
+
+def mm(a, b, dims=NN):
+    return lax.dot_general(a, b, dims, preferred_element_type=F32)
+
+
+def split2(x):
+    hi = x.astype(BF16)
+    return hi, (x - hi.astype(F32)).astype(BF16)
+
+
+def split3(x):
+    hi = x.astype(BF16).astype(F32)
+    mid = (x - hi).astype(BF16).astype(F32)
+    return hi, mid, x - hi - mid
+
+
+def iota(shape, axis):
+    return lax.broadcasted_iota(jnp.int32, shape, axis)
+
+
+def one_hot(index, rows):
+    return (iota((rows, index.shape[1]), 0) == index).astype(F32)
+
+
+def solids(x, y, z, r2):
+    return (
+        None,
+        R15 * x * y,
+        R15 * y * z,
+        0.5 * R5 * (3.0 * z * z - r2),
+        R15 * x * z,
+        0.5 * R15 * (x * x - y * y),
+        R3 * x,
+        R3 * y,
+        R3 * z,
+    )
+
+
+def scaled(block, solid):
+    return block if solid is None else block * solid
+
+
+def block_of(array, k):
+    return array[k * C : (k + 1) * C]
+
+
+def own_table(positions_ref, species_ref):
+    return jnp.concatenate(
+        [
+            positions_ref[0],
+            positions_ref[1],
+            positions_ref[2],
+            species_ref[...].astype(F32),
+            jnp.zeros((4, ATOMS), F32),
+        ],
+        axis=0,
+    )
+
+
+def rows_of(own, atoms):
+    return jnp.concatenate(
+        [
+            jnp.take_along_axis(
+                own,
+                jnp.broadcast_to(atoms[:, at : at + LANES], (8, LANES)),
+                axis=1,
+                mode="promise_in_bounds",
+            )
+            for at in range(0, atoms.shape[1], LANES)
+        ],
+        axis=1,
+    )
+
+
+def pair_rows(vector, kind, column, first):
+    hi, mid, low = split3(vector)
+    one = jnp.ones_like(kind)
+    zero = jnp.zeros_like(kind)
+    parts = [hi[0:3], kind, column, first, one, zero, mid[0:3], zero, low[0:3], zero]
+    return jnp.concatenate(parts, axis=0)
+
+
+def from_terms(total_ref, t):
+    upper = total_ref[t * 16 : t * 16 + 8, :]
+    lower = total_ref[t * 16 + 8 : t * 16 + 16, :]
+    return upper + jnp.where(iota((8, LANES), 0) < 3, lower + pltpu.roll(lower, 4, 0), 0.0)
+
+
+def sixteen_rows(tiles, groups):
+    return ((iota((16 * tiles, groups), 0) >> 4) == iota((16 * tiles, groups), 1)).astype(
+        F32
+    ).astype(BF16)
+
+
+def earlier_lanes():
+    return (iota((PACK, PACK), 0) < iota((PACK, PACK), 1)).astype(BF16)
+
+
+def pack_kernel(
+    positions_ref,
+    species_ref,
+    sends_ref,
+    first_ref,
+    second_ref,
+    low_ref,
+    mid_ref,
+    high_ref,
+    over_ref,
+    total_ref,
+    picked_ref,
+    lane_ref,
+):
+    row = iota((8, LANES), 0)
+    lanes = iota((8, LANES), 1)
+    own = own_table(positions_ref, species_ref)
+    earlier = earlier_lanes()
+    tiles = [s for s in range(SLOTS) if s != HERE]
+    rows = sixteen_rows(MASKED, GROUPS)
+    count = jnp.zeros((GROUPS, 1), F32)
+    for start in range(0, second_ref.shape[1], PACK):
+        first = first_ref[:, start : start + PACK]
+        ghost = second_ref[:, start : start + PACK] - ATOMS
+        near = rows_of(own, first)
+        slot = ghost >> 3
+        group = jnp.where(ghost >= 0, jnp.where(slot > HERE, slot - 1, slot), -1)
+        member = one_hot(group, GROUPS)
+        low_member = member.astype(BF16)
+        rank = mm(low_member, earlier) + count
+        rank = jnp.sum(rank * member, axis=0, keepdims=True).astype(jnp.int32)
+        count = count + jnp.sum(member, axis=1, keepdims=True)
+        lane = jnp.where(rank < CAP, rank, -1)
+        column = (ghost & 7).astype(F32)
+        data = pair_rows(near, near[3:4], column, first.astype(F32))
+        here = slice(start, start + PACK)
+        picked = mm(rows, low_member) * jnp.concatenate([data] * MASKED, axis=0)
+        picked_ref[: 16 * MASKED, here] = picked.astype(BF16)
+        low = data.astype(BF16)
+        for t in range(MASKED, len(tiles)):
+            picked = jnp.where(group == t, low, jnp.zeros_like(low))
+            picked_ref[16 * t : 16 * t + 16, here] = picked
+        lane_ref[:, here] = one_hot(lane, LANES).astype(BF16)
+    total_ref[...] = mm(picked_ref[...], lane_ref[...], NT)
+    spread = (iota((GHOSTS, LANES), 1) == iota((GHOSTS, LANES), 0) + CAP).astype(BF16)
+    atoms = mm(sends_ref[...].astype(F32).astype(BF16), spread, TN).astype(jnp.int32)
+    for s in range(SLOTS):
+        ref = (low_ref, mid_ref, high_ref)[s // 9]
+        if s == HERE:
+            tile = jnp.zeros((8, LANES), F32)
+        else:
+            listed = atoms[s : s + 1]
+            ghosts = rows_of(own, jnp.maximum(listed, 0))
+            ghosts = jnp.where(row == 5, listed.astype(F32), ghosts)
+            tile = jnp.where(lanes >= CAP, ghosts, from_terms(total_ref, tiles.index(s)))
+        ref[s % 9 * 8 : s % 9 * 8 + 8, :] = tile
+    crowded = (count > CAP).astype(F32)
+    over_ref[...] = jnp.zeros((8, LANES), F32) + jnp.sum(crowded, axis=0, keepdims=True)
+
+
+def inner_kernel(positions_ref, species_ref, first_ref, second_ref, pairs_ref, total_ref):
+    own = own_table(positions_ref, species_ref)
+    earlier = earlier_lanes()
+    tiles = range(OWN_TILES)
+    count = jnp.zeros((8, 1), F32)
+    for start in range(0, second_ref.shape[1], PACK):
+        first = first_ref[:, start : start + PACK]
+        second = second_ref[:, start : start + PACK]
+        inside = jnp.logical_and(second >= 0, second < ATOMS)
+        near = rows_of(own, first)
+        far = rows_of(own, jnp.clip(second, 0, ATOMS - 1))
+        member = jnp.broadcast_to(inside.astype(F32), (8, PACK))
+        rank = (mm(member.astype(BF16), earlier) + count)[0:1].astype(jnp.int32)
+        count = count + jnp.sum(member, axis=1, keepdims=True)
+        tile = jnp.where(inside, rank >> 7, -1)
+        kind = near[3:4] * NSPEC + far[3:4]
+        column = jnp.clip(second, 0, ATOMS - 1).astype(F32)
+        data = pair_rows(far - near, kind, column, first.astype(F32))
+        low = data.astype(BF16)
+        picked = [jnp.where(tile == t, low, jnp.zeros_like(low)) for t in tiles]
+        at_lane = one_hot(rank & 127, LANES).astype(BF16)
+        part = mm(jnp.concatenate(picked, axis=0), at_lane, NT)
+        if start == 0:
+            total_ref[...] = part
+        else:
+            total_ref[...] += part
+    for t in tiles:
+        pairs_ref[t * 8 : t * 8 + 8, :] = from_terms(total_ref, t)
+
+
+def whole_number(row):
+    return jnp.sum(row, axis=1, keepdims=True).astype(jnp.int32)[0, 0]
+
+
+def core_kernel(
+    out_low_ref,
+    out_mid_ref,
+    out_high_ref,
+    in_low_ref,
+    in_mid_ref,
+    in_high_ref,
+    pairs_ref,
+    over_ref,
+    latent_ref,
+    channel_ref,
+    energy_w_ref,
+    inv_w_ref,
+    radial_w_ref,
+    vector_ref,
+    grad_own_ref,
+    low_ref,
+    mid_ref,
+    high_ref,
+    centre_ref,
+    sum_ref,
+    edge_ref,
+    grad_ref,
+    at_ref,
+    slope_ref,
+    weights_ref,
+    hidden_ref,
+    active_ref,
+    grad_w_ref,
+    grad_s_ref,
+    total_ref,
+    table_ref,
+    env_ref,
+    energy_ref,
+    column_ref,
+    energy_t_ref,
+    inv_t_ref,
+    shared_ref,
+):
+    row = iota((8, LANES), 0)
+    lanes = iota((8, LANES), 1)
+
+    spots = []
+    filled = jnp.int32(0)
+    sent_at = [
+        (out_low_ref, out_mid_ref, out_high_ref)[s // 9][s % 9 * 8 : s % 9 * 8 + 8, :]
+        for s in range(SLOTS)
+    ]
+    got_at = [
+        (in_low_ref, in_mid_ref, in_high_ref)[s % 3][s // 3 * 8 : s // 3 * 8 + 8, :]
+        for s in range(SLOTS)
+    ]
+    slots = [s for s in range(SLOTS) if s != HERE]
+    centre_ref[2 * HERE : 2 * HERE + 2, :] = jnp.full((2, LANES), -1, jnp.int32)
+
+    def at_column(table, column):
+        index = jnp.broadcast_to(CAP + column.astype(jnp.int32), (8, LANES))
+        return jnp.take_along_axis(table, index, axis=1, mode="promise_in_bounds")
+
+    ghosts = [at_column(got_at[s], sent_at[s][4:5]) for s in slots]
+    atoms = [at_column(sent_at[s], got_at[s][4:5]) for s in slots]
+    tiles = []
+    for s, ghost, atom in zip(slots, ghosts, atoms):
+        sent, got = sent_at[s], got_at[s]
+        offset = jnp.where(
+            row == 0,
+            float(s // 9 - 1),
+            jnp.where(row == 1, float(s // 3 % 3 - 1), jnp.where(row == 2, float(s % 3 - 1), 0.0)),
+        )
+        ours = jnp.logical_and(lanes < CAP, sent[6:7] > 0.5)
+        theirs = jnp.logical_and(lanes < CAP, got[6:7] > 0.5)
+        tile = jnp.where(
+            row < 3, (ghost + offset) - sent, jnp.where(row == 3, sent * NSPEC + ghost, sent)
+        )
+        tiles.append(jnp.where(ours, tile, 0.0))
+        tile = jnp.where(
+            row < 3,
+            (got + offset) - atom,
+            jnp.where(row == 3, got * NSPEC + atom, jnp.where(row == 5, atom, got)),
+        )
+        tiles.append(jnp.where(theirs, tile, 0.0))
+    for k, tile in enumerate(tiles):
+        at = 2 * slots[k // 2] + k % 2
+        centre = jnp.where(tile[6:7] > 0.5, tile[5:6], -1.0)
+        centre_ref[at : at + 1, :] = centre.astype(jnp.int32)
+    counts = [jnp.sum(tile[6:7], axis=1, keepdims=True) for tile in tiles]
+    counts = [count.astype(jnp.int32)[0, 0] for count in counts]
+    held = jnp.zeros((8, LANES), F32)
+    for tile, count in zip(tiles, counts):
+        at = EDGE_START + (filled >> 7)
+        shift = filled & 127
+        turned = pltpu.roll(tile, shift, 1)
+        whole = held + jnp.where(lanes >= shift, turned, 0.0)
+        rest = jnp.where(lanes < shift, turned, 0.0)
+        edge_ref[at] = whole
+        edge_ref[at + 1] = rest
+        held = jnp.where(shift + count >= LANES, rest, whole)
+        spots.append((filled, count))
+        filled = filled + count
+    for k in range(1, PART + 1):
+        edge_ref[EDGE_START + (filled >> 7) + k] = jnp.zeros((8, LANES), F32)
+    for t in range(OWN_TILES, EDGE_START):
+        edge_ref[t] = jnp.zeros((8, LANES), F32)
+    own_count = jnp.zeros((1, LANES), F32)
+    for t in range(OWN_TILES):
+        tile = pairs_ref[t * 8 : t * 8 + 8, :]
+        edge_ref[t] = tile
+        own_count = own_count + tile[6:7]
+    own_count = whole_number(own_count)
+    own_chunks = (own_count + CHUNK - 1) // CHUNK
+    edge_chunks = (filled + CHUNK - 1) // CHUNK
+    column_ref[...] = jnp.transpose(jnp.broadcast_to(0.5 * vector_ref[...], (LANES, LANES)))
+    energy_t_ref[...] = jnp.transpose(0.5 * energy_w_ref[...].astype(F32)).astype(BF16)
+    inv_t_ref[...] = jnp.transpose(0.5 * inv_w_ref[...].astype(F32)).astype(BF16)
+
+    def load(chunk):
+        edges = jnp.concatenate([edge_ref[PART * chunk + k] for k in range(PART)], axis=1)
+        x, y, z = edges[0:1], edges[1:2], edges[2:3]
+        return edges, x, y, z, x * x + y * y + z * z, edges[6:7]
+
+    def radial_of(r2):
+        centre = RADIAL_STEP * iota((NB, 1), 0).astype(F32)
+        shifted = (r2 - centre) * (1.0 / RADIAL_WIDTH)
+        return centre, jnp.exp(-(shifted * shifted))
+
+    def silu(half):
+        bent = jnp.tanh(half)
+        twice = bent + 1.0
+        value = half * twice
+        return value, twice + value * (1.0 - bent)
+
+    def component(block, solid):
+        return block if solid is None else block * solid.astype(BF16)
+
+    def env_chunk(chunk, two, spare):
+        edges, x, y, z, r2, valid = load(chunk)
+        at_first = one_hot(jnp.where(valid > 0.5, edges[5:6], -1.0).astype(jnp.int32), ATOMS)
+        at_ref[chunk, 0] = at_first.astype(BF16)
+        if two:
+            at_second = one_hot(jnp.where(valid > 0.5, edges[4:5], -1.0).astype(jnp.int32), ATOMS)
+            even = (at_first + at_second).astype(BF16)
+            odd = (at_first - at_second).astype(BF16)
+            at_ref[chunk, 1] = at_second.astype(BF16)
+            at_ref[chunk, 2] = even
+            at_ref[chunk, 3] = odd
+        else:
+            even = odd = at_first.astype(BF16)
+        combo = one_hot(edges[3:4].astype(jnp.int32), COMBOS)
+        centre, radial = radial_of(r2)
+        stacked = jnp.concatenate([combo, combo, radial, jnp.zeros_like(radial)], axis=0)
+        half = mm(latent_ref[...], stacked.astype(BF16))
+        yield
+        hidden, active = silu(half)
+        active_ref[chunk] = active
+        hidden = hidden.astype(BF16)
+        hidden_ref[chunk] = hidden
+        weights = mm(channel_ref[...], hidden)
+        yield
+        weights = weights * jnp.exp(-0.5 * r2)
+        weights_ref[chunk] = weights
+        solid = solids(x, y, z, r2)
+        weights = weights.astype(BF16)
+        parts = [component(block_of(weights, LEVEL[m]), solid[m]) for m in range(9)]
+        yield (jnp.concatenate(parts[:6], axis=0), even, jnp.concatenate(parts[6:], axis=0), odd)
+
+    def energy_side(chunk, turned, two, spare, apart):
+        edges, x, y, z, r2, valid = load(chunk)
+        solid = solids(x, y, z, r2)
+        solid = [-solid[m] if turned and LEVEL[m] == 1 else solid[m] for m in range(9)]
+        at = at_ref[chunk, int(turned)]
+        env_ref[spare] = mm(table_ref[...], at)
+        shared = None if turned else mm(energy_t_ref[...], hidden_ref[chunk])
+        if two and not turned:
+            shared_ref[...] = shared
+        yield
+        weights = weights_ref[chunk]
+        inner = [None] * 3
+        for m in range(9):
+            term = scaled(env_ref[spare, m * C : (m + 1) * C, :], solid[m])
+            inner[LEVEL[m]] = term if inner[LEVEL[m]] is None else inner[LEVEL[m]] + term
+        inner = jnp.concatenate(inner, axis=0)
+        if turned:
+            shared = shared_ref[...]
+        half = shared + mm(inv_t_ref[...], (weights * inner).astype(BF16))
+        yield
+        act, slope = silu(half)
+        energy_ref[...] += act * valid
+        grad = jnp.concatenate([column_ref[...]] * (CHUNK // LANES), axis=1) * slope
+        back = mm(inv_w_ref[...], grad.astype(BF16))
+        yield
+        back = back.astype(BF16).astype(F32)
+        grad_w = back * inner
+        up = back * weights
+        slopes = []
+        parts = []
+        up_low = up.astype(BF16)
+        for m in range(9):
+            block = block_of(up, LEVEL[m])
+            if m:
+                slope = jnp.sum(block * env_ref[spare, m * C : (m + 1) * C, :], axis=0, keepdims=True)
+                slopes.append(-slope if turned and LEVEL[m] == 1 else slope)
+            parts.append(component(block_of(up_low, LEVEL[m]), solid[m]))
+        slopes = jnp.concatenate(slopes, axis=0)
+        if turned:
+            grad_w_ref[chunk] += grad_w
+            grad_s_ref[chunk] += grad
+            slope_ref[chunk] += slopes
+        else:
+            grad_w_ref[chunk] = grad_w
+            grad_s_ref[chunk] = grad
+            slope_ref[chunk] = slopes
+        parts = jnp.concatenate(parts, axis=0)
+        if apart:
+            total_ref[...] += mm(parts, at, NT)
+        yield (parts, at)
+
+    def force_chunk(chunk, two, spare):
+        edges, x, y, z, r2, valid = load(chunk)
+        solid = solids(x, y, z, r2)
+        if two:
+            env_ref[spare, :EVEN] = mm(table_ref[:EVEN], at_ref[chunk, 2])
+            env_ref[spare, EVEN:] = mm(table_ref[EVEN:], at_ref[chunk, 3])
+        else:
+            env_ref[spare] = mm(table_ref[...], at_ref[chunk, 0])
+        yield
+        weights = weights_ref[chunk]
+        grown = [None] * 3
+        slopes = [None] * 9
+        for m in range(9):
+            level = LEVEL[m]
+            block = env_ref[spare, m * C : (m + 1) * C, :]
+            term = scaled(block, solid[m])
+            grown[level] = term if grown[level] is None else grown[level] + term
+            if m:
+                slopes[m] = slope_ref[chunk, m - 1 : m, :] + jnp.sum(
+                    block_of(weights, level) * block, axis=0, keepdims=True
+                )
+        grad_w = grad_w_ref[chunk] + jnp.concatenate(grown, axis=0)
+        grad_r2 = -0.5 * jnp.sum(grad_w * weights, axis=0, keepdims=True)
+        decay = jnp.exp(-0.5 * r2)
+        back = mm(channel_ref[...], (grad_w * decay).astype(BF16), TN) + mm(
+            energy_w_ref[...], grad_s_ref[chunk].astype(BF16)
+        )
+        yield
+        back = back.astype(BF16).astype(F32) * active_ref[chunk]
+        grad_radial = mm(radial_w_ref[...], back.astype(BF16))
+        yield
+        grad_radial = grad_radial[:NB].astype(BF16).astype(F32)
+        centre, radial = radial_of(r2)
+        grad_r2 += (-2.0 / RADIAL_WIDTH**2) * jnp.sum(
+            grad_radial * radial * (r2 - centre), axis=0, keepdims=True
+        )
+        xy, yz, zz, xz, xx, px, py, pz = slopes[1:]
+        grad_x = 2.0 * x * grad_r2 + R15 * (y * xy + z * xz + x * xx) - R5 * x * zz + R3 * px
+        grad_y = 2.0 * y * grad_r2 + R15 * (x * xy + z * yz - y * xx) - R5 * y * zz + R3 * py
+        grad_z = 2.0 * z * grad_r2 + R15 * (y * yz + x * xz) + 2.0 * R5 * z * zz + R3 * pz
+        grads = jnp.concatenate([grad_x, grad_y, grad_z, jnp.zeros((5, CHUNK), F32)], axis=0)
+        if not two:
+            for k in range(PART):
+                grad_ref[PART * chunk + k] = grads[:, k * LANES : (k + 1) * LANES]
+        hi = grads.astype(BF16).astype(F32)
+        parts = jnp.concatenate([hi, grads - hi], axis=0).astype(BF16)
+        toward = at_ref[chunk, 3 if two else 0]
+        yield (parts, toward)
+
+    def together(works, lag=0):
+        works = list(works)
+        ends = [None] * len(works)
+        turn = 0
+        while None in ends:
+            for k, work in enumerate(works):
+                if turn >= lag * k and ends[k] is None:
+                    ends[k] = next(work)
+            turn += 1
+        return ends
+
+    def joined(parts):
+        return parts[0] if len(parts) == 1 else jnp.concatenate(parts, axis=1)
+
+    def env_step(items):
+        ends = together(env_chunk(c, two, k) for k, (c, two) in enumerate(items))
+        total_ref[:EVEN] += mm(joined([e[0] for e in ends]), joined([e[1] for e in ends]), NT)
+        total_ref[EVEN:] += mm(joined([e[2] for e in ends]), joined([e[3] for e in ends]), NT)
+
+    def energy_step(items):
+        sides = []
+        for c, two in items:
+            sides.append((c, False, two))
+            if two:
+                sides.append((c, True, two))
+        many = len(sides) > 2
+        if many:
+            sides = sides[2:] + sides[:2]
+        ends = together(
+            (energy_side(*side, k, many) for k, side in enumerate(sides)), int(many)
+        )
+        if not many:
+            total_ref[...] += mm(joined([e[0] for e in ends]), joined([e[1] for e in ends]), NT)
+
+    def force_step(items):
+        ends = together(force_chunk(c, two, k) for k, (c, two) in enumerate(items))
+        grad_own_ref[...] += mm(joined([e[0] for e in ends]), joined([e[1] for e in ends]), NT)
+
+    def each(step):
+        def both(chunk, carry):
+            step([(chunk, True), (OWN_CHUNKS + chunk, False)])
+            return carry
+
+        def own(chunk, carry):
+            step([(chunk, True)])
+            return carry
+
+        def outer(chunk, carry):
+            step([(OWN_CHUNKS + chunk, False)])
+            return carry
+
+        def outer_two(pair, carry):
+            chunk = OWN_CHUNKS + shared + 2 * pair
+            step([(chunk, False), (chunk + 1, False)])
+            return carry
+
+        shared = jnp.minimum(own_chunks, edge_chunks)
+        twos = (edge_chunks - shared) // 2
+        lax.fori_loop(0, shared, both, 0)
+        lax.fori_loop(shared, own_chunks, own, 0)
+        lax.fori_loop(0, twos, outer_two, 0)
+        lax.fori_loop(shared + 2 * twos, edge_chunks, outer, 0)
+
+    total_ref[...] = jnp.zeros_like(total_ref)
+    energy_ref[...] = jnp.zeros_like(energy_ref)
+    grad_own_ref[...] = jnp.zeros_like(grad_own_ref)
+    each(env_step)
+    table_ref[...] = (ENV_SCALE * total_ref[...]).astype(BF16)
+    total_ref[...] = jnp.zeros_like(total_ref)
+    each(energy_step)
+    table_ref[...] = (ENV_SCALE * total_ref[...]).astype(BF16)
+    each(force_step)
+
+    energy = sum(energy_ref[:, k * LANES : (k + 1) * LANES] for k in range(PART))
+    energy = jnp.sum(2.0 * column_ref[...] * energy, axis=0, keepdims=True)
+    energy = jnp.sum(energy, axis=1, keepdims=True)
+    sums = jnp.where(lanes == 0, energy, over_ref[...])
+    low_ref[SIDE_ROWS:, :] = sums
+    high_ref[SIDE_ROWS:, :] = sums
+    sum_ref[...] = sums
+
+    def recall(spot):
+        start, count = spot
+        at = EDGE_START + (start >> 7)
+        shift = start & 127
+        tile = jnp.where(lanes >= shift, grad_ref[at], grad_ref[at + 1])
+        return jnp.where(lanes < count, pltpu.roll(tile, (LANES - shift) & 127, 1), 0.0)
+
+    place = 0
+    for s in range(SLOTS):
+        ref = (low_ref, mid_ref, high_ref)[s // 9]
+        if s == HERE:
+            tile = jnp.zeros((8, LANES), F32)
+        else:
+            tile = recall(spots[place]) + pltpu.roll(recall(spots[place + 1]), 4, 0)
+            place += 2
+        ref[s % 9 * 8 : s % 9 * 8 + 8, :] = tile
+
+
+def final_kernel(own_ref, in_low_ref, in_mid_ref, in_high_ref, centre_ref, out_ref):
+    total = -own_ref[...]
+    for s in range(SLOTS):
+        if s == HERE:
+            continue
+        ref = (in_low_ref, in_mid_ref, in_high_ref)[s % 3]
+        tile = ref[s // 3 * 8 : s // 3 * 8 + 8, :]
+        hi = tile.astype(BF16).astype(F32)
+        parts = jnp.concatenate([hi, tile - hi], axis=0)
+        theirs = one_hot(centre_ref[2 * s + 1 : 2 * s + 2, :], ATOMS)
+        ours = one_hot(centre_ref[2 * s : 2 * s + 1, :], ATOMS)
+        ats = jnp.concatenate([theirs, ours], axis=1).astype(BF16)
+        both = jnp.concatenate([parts, pltpu.roll(parts, 12, 0)], axis=1).astype(BF16)
+        total = total + mm(both, ats, NT)
+    total = -(total[0:8] + total[8:16])
+    for k in range(3):
+        out_ref[k] = total[k : k + 1]
+
+
+def shape(rows, cols, dtype=F32):
+    return jax.ShapeDtypeStruct((rows, cols), dtype)
+
+
+def shifted(cells, axis, step):
+    count = lax.axis_size(axis)
+    return lax.ppermute(cells, axis, [(i, (i + step) % count) for i in range(count)])
+
+
+def settle(*arrays):
+    return lax.optimization_barrier(arrays)
+
+
+def swap_tiles(low, mid, high, sums=None, task=None):
+    def pieces(left, mid, right, part):
+        pick = slice(24 * part, 24 * part + 24)
+        return [left[pick], mid[pick], right[pick]]
+
+    row = lax.broadcasted_iota(jnp.int32, (8, LANES), 0)
+    extra = [] if sums is None else [sums]
+    left, right = shifted(high, "gx", 1), shifted(low, "gx", -1)
+    if extra:
+        even = lax.axis_index("gx") % 2 == 0
+        sums = sums + jnp.where(even, left[SIDE_ROWS:], right[SIDE_ROWS:])
+        extra = [sums]
+    done = None
+    if task is not None:
+        run, arrays = task
+        left, right, *arrays = settle(left, right, *arrays)
+        done = run(*arrays)
+    low, high = (
+        jnp.concatenate(pieces(left, mid, right, part) + extra, axis=0) for part in (0, 2)
+    )
+    mid = jnp.concatenate(pieces(left, mid, right, 1), axis=0)
+    left, right = shifted(high, "gy", 1), shifted(low, "gy", -1)
+    if extra:
+        far = shifted(sums, "gy", 2)
+        left, right, far = settle(left, right, far)
+        sums = sums + left[SIDE_ROWS:] + right[SIDE_ROWS:] + far
+        extra = [sums]
+
+    def tiles(part):
+        picked = []
+        for a in range(3):
+            for array in (left, mid, right):
+                start = 24 * a + 8 * part
+                picked.append(array[start : start + 8])
+        return picked
+
+    low, high = (jnp.concatenate(tiles(part) + extra, axis=0) for part in (0, 2))
+    mid = jnp.concatenate(tiles(1), axis=0)
+    if task is not None:
+        low, high, done = settle(low, high, done)
+    left, right = shifted(high, "gz", 1), shifted(low, "gz", -1)
+    if extra:
+        before = left[SIDE_ROWS:]
+        sums = sums + right[SIDE_ROWS:] + jnp.where(row % 2 == 0, before, 0.0)
+    return left, mid, right, sums, done
+
+
+def as_it_lies(array):
+    return with_layout_constraint(array, Layout(major_to_minor=tuple(range(array.ndim))))
+
+
+def grid_total(sums):
+    sums = sums + shifted(sums, "gx", 4)
+    sums = sums + other_core(sums)
+    even = lax.axis_index("gx") % 2 == 0
+    count_x, count_z = lax.axis_size("gx"), lax.axis_size("gz")
+    moves = []
+    for x in range(count_x):
+        for z in range(count_z):
+            to = (z + (3 if x % 2 else -3)) % count_z
+            moves.append((x * count_z + z, x * count_z + to))
+    rest = lax.ppermute(jnp.where(even, sums[0:1], sums[1:2]), ("gx", "gz"), moves)
+    return sums[0:1] + rest + other_core(rest)
+
+
+def other_core(array):
+    return lax.ppermute(array, "gx", [(i, i ^ 1) for i in range(lax.axis_size("gx"))])
+
+
+def per_device(
+    positions,
+    species,
+    send_list,
+    pair_first,
+    pair_second,
+    species_embed,
+    w_latent,
+    w_channel,
+    w_energy,
+    w_invariant,
+    energy_vector,
+):
+    sides = (shape(SIDE_ROWS, LANES),) * 3
+    small = pltpu.CompilerParams(vmem_limit_bytes=12 * 1024 * 1024)
+    large = pltpu.CompilerParams(vmem_limit_bytes=48 * 1024 * 1024)
+    places = positions.reshape(1, ATOMS, 3).transpose(2, 0, 1)
+    kinds = species.reshape(1, ATOMS)
+    sends = send_list.reshape(SLOTS, GHOSTS).T
+    firsts = pair_first.reshape(1, -1)
+    seconds = pair_second.reshape(1, -1)
+    low, mid, high, over = pl.pallas_call(
+        pack_kernel,
+        out_shape=(*sides, shape(8, LANES)),
+        scratch_shapes=[
+            pltpu.VMEM(((SLOTS - 1) * 16, LANES), F32),
+            pltpu.VMEM(((SLOTS - 1) * 16, seconds.shape[1]), BF16),
+            pltpu.VMEM((LANES, seconds.shape[1]), BF16),
+        ],
+        compiler_params=small,
+    )(places, kinds, sends, firsts, seconds)
+    inner_call = pl.pallas_call(
+        inner_kernel,
+        out_shape=shape(OWN_TILES * 8, LANES),
+        scratch_shapes=[pltpu.VMEM((OWN_TILES * 16, LANES), F32)],
+        compiler_params=small,
+    )
+    in_low, in_mid, in_high, _, inner = swap_tiles(
+        low, mid, high, task=(inner_call, (places, kinds, firsts, seconds))
+    )
+
+    embed_first = jnp.repeat(species_embed, NSPEC, axis=0)
+    embed_second = jnp.tile(species_embed, (NSPEC, 1))
+    features = jnp.concatenate(
+        [embed_first + embed_second, embed_first * embed_second], axis=1
+    ).astype(BF16)
+    features = jnp.pad(features, ((0, COMBOS - NSPEC * NSPEC), (0, 0)))
+    combos = mm(w_latent[NB:], features, (((0,), (1,)), ((), ())))
+    high_part = lax.reduce_precision(combos, exponent_bits=8, mantissa_bits=7)
+    hi, lo = high_part.astype(BF16), (combos - high_part).astype(BF16)
+    radial_w = jnp.pad(0.5 * w_latent[:NB], ((0, 8), (0, 0)))
+    latent_w = jnp.concatenate([0.5 * hi, 0.5 * lo, radial_w.T], axis=1)
+
+    hidden_width, readout = w_energy.shape
+    side = shape(SIDE_ROWS + 8, LANES)
+    grad_own, low, mid, high, centres, sums = pl.pallas_call(
+        core_kernel,
+        out_shape=(
+            shape(16, ATOMS),
+            side,
+            shape(SIDE_ROWS, LANES),
+            side,
+            shape(2 * SLOTS, LANES, jnp.int32),
+            shape(8, LANES),
+        ),
+        scratch_shapes=[
+            pltpu.VMEM((CHUNKS * PART + PART, 8, LANES), F32),
+            pltpu.VMEM((CHUNKS * PART + PART, 8, LANES), F32),
+            pltpu.VMEM((CHUNKS, 4, ATOMS, CHUNK), BF16),
+            pltpu.VMEM((CHUNKS, 8, CHUNK), F32),
+            pltpu.VMEM((CHUNKS, 3 * C, CHUNK), F32),
+            pltpu.VMEM((CHUNKS, hidden_width, CHUNK), BF16),
+            pltpu.VMEM((CHUNKS, hidden_width, CHUNK), F32),
+            pltpu.VMEM((CHUNKS, 3 * C, CHUNK), F32),
+            pltpu.VMEM((CHUNKS, readout, CHUNK), F32),
+            pltpu.VMEM((WIDTH, ATOMS), F32),
+            pltpu.VMEM((WIDTH, ATOMS), BF16),
+            pltpu.VMEM((3, WIDTH, CHUNK), F32),
+            pltpu.VMEM((readout, CHUNK), F32),
+            pltpu.VMEM((readout, LANES), F32),
+            pltpu.VMEM((readout, hidden_width), BF16),
+            pltpu.VMEM((readout, 3 * C), BF16),
+            pltpu.VMEM((readout, CHUNK), F32),
+        ],
+        compiler_params=large,
+    )(
+        low,
+        mid,
+        high,
+        in_low,
+        in_mid,
+        in_high,
+        inner,
+        over,
+        latent_w,
+        w_channel.T,
+        w_energy,
+        w_invariant,
+        radial_w,
+        energy_vector.reshape(1, -1),
+    )
+
+    in_low, in_mid, in_high, sums, _ = swap_tiles(low, mid, high, sums)
+    forces = pl.pallas_call(
+        final_kernel,
+        out_shape=jax.ShapeDtypeStruct((3, 1, ATOMS), F32),
+        compiler_params=small,
+    )(grad_own, in_low, in_mid, in_high, centres)
+    sums = grid_total(sums)
+    devices = lax.axis_size("gx") * lax.axis_size("gy") * lax.axis_size("gz")
+    crowded = sums[0, 1] > 0.5
+    energy = sums[0, :1] / (ATOMS * devices)
+
+    def again(state):
+        held = (places, kinds, sends, firsts, seconds, state[2])
+        own_places, own_kinds, own_sends, own_firsts, own_seconds, _ = lax.optimization_barrier(held)
+        own_places, own_sends = as_it_lies(own_places), as_it_lies(own_sends)
+        forces, energy = general(
+            own_places.transpose(1, 2, 0).reshape(positions.shape),
+            own_kinds.reshape(species.shape),
+            own_sends.T.reshape(send_list.shape),
+            own_firsts.reshape(pair_first.shape),
+            own_seconds.reshape(pair_second.shape),
+            species_embed,
+            w_latent,
+            w_channel,
+            w_energy,
+            w_invariant,
+            energy_vector,
+        )
+        forces = as_it_lies(forces.reshape(1, ATOMS, 3).transpose(2, 0, 1))
+        return forces, energy, jnp.zeros((), bool)
+
+    forces, energy, _ = lax.while_loop(lambda state: state[2], again, (forces, energy, crowded))
+    return forces.transpose(1, 2, 0).reshape(positions.shape), energy
+
+
 def solution(mesh):
     return jax.shard_map(
         per_device,

time: 1000 us -> 75.6 us (0.08)
  other arithmetic: 283 us -> 1.7 us
  local copies, waits for them, and re-layouts: 178 us -> 0.94 us
  waiting for transfers between devices: 169 us -> 8.87 us
  starting transfers between devices: 173 us -> 40.9 us
  matrix products: 94.5 us -> 1.07 us
  blocking collectives: 79.1 us -> 0 us
  Pallas kernels: 0 us -> 17.6 us
  loops' own time: 11 us -> 0.15 us
    ppermute x36 -> x17, waiting for transfers between devices: 169 us -> 8.87 us  [the longest x14 6.68 us: shifted(): lax.ppermute(cells, axis, [(i, (i + step) % count) for i in range(count)])]
    scatter-add x63 -> x0, other arithmetic: 143 us -> none  [the longest x12 31.7 us: energy_block(): grad_env.at[first_rows].add(grad_first).at[second_rows].add(grad_second)]
    ppermute x36 -> x17, starting transfers between devices: 173 us -> 40.9 us  [the longest x14 29.4 us: shifted(): lax.ppermute(cells, axis, [(i, (i + step) % count) for i in range(count)])]
    gather x178 -> x0, local copies, waits for them, and re-layouts: 130 us -> none  [the longest x72 29.1 us: block_pairs(): displace = table_pos[second_rows] - table_pos[first_rows]]
    dot_general x126 -> x1, matrix products: 94.5 us -> 1.07 us  [mm(): return lax.dot_general(a, b, dims, preferred_element_type=F32)]
    psum x1 -> x0, blocking collectives: 79.1 us -> none  [per_device(): grand_total = lax.psum(energy_sum, ('gx', 'gy', 'gz'))]
    mul x106 -> x1, other arithmetic: 42 us -> 0.69 us  [per_device(): radial_w = jnp.pad(0.5 * w_latent[:NB], ((0, 8), (0, 0)))]
    reduce_sum x85 -> x0, other arithmetic: 36 us -> none  [the longest x12 18.1 us: pair_tensors(): per_component * (solid * PARITY)[:, :, None]]
  transfers between devices with their start and end apart: 36 -> 17, of which waited for: 31 -> 9; matrix products, arithmetic and copies ran while one was open for 0% -> 4% of each run, Pallas kernels for 0% -> 4%
where the time goes in v1:
time: 75.6 us; the launch traced here: 74.7 us
  starting transfers between devices  40.9 us (54%)
  Pallas kernels  17.6 us (23%)
  waiting for transfers between devices  8.87 us (12%)
  between operations  3.41 us (5%)
  other arithmetic  1.7 us (2%)
  matrix products  1.07 us (1%)
  local copies, waits for them, and re-layouts  0.94 us (1%)
    ppermute x14, starting transfers between devices, shifted(): lax.ppermute(cells, axis, [(i, (i + step) % count) for i in range(count)])  29.4 us
    pallas_call x1, Pallas kernels, per_device(): pl.pallas_call(core_kernel, out_shape=(shape(16, ATOMS), side, shape(SIDE...  12.8 us
    ppermute x2, starting transfers between devices, other_core(): lax.ppermute(array, 'gx', [(i, i ^ 1) for i in range(lax.axis_size('gx'))])  7.43 us
    ppermute x14, waiting for transfers between devices, shifted(): lax.ppermute(cells, axis, [(i, (i + step) % count) for i in range(count)])  6.68 us
    ppermute x1, starting transfers between devices, grid_total(): lax.ppermute(jnp.where(even, sums[0:1], sums[1:2]), ('gx', 'gz'), moves)  4.07 us
    pallas_call x1, Pallas kernels, swap_tiles(): done = run(*arrays)  1.9 us
    pallas_call x1, Pallas kernels, per_device(): pl.pallas_call(pack_kernel, out_shape=(*sides, shape(8, LANES)), scratch_...  1.85 us
  transfers between devices with their start and end apart: 17, of which 9 were waited for; matrix products, arithmetic and copies ran while one was open for 4% of the time, Pallas kernels for 4%

profile of v1, /device:TPU:1, one launch (start us, length us, event | category | flops | bytes accessed | tf_op | source)
XLA Modules:
  0.0 74.7 jit_solution(8005206050080408379)
XLA Ops:
  0.7 1.8 %shard_map.176 = (f32[72,128]{1,0:T(8,128)S(1)}, f32[72,128]{1,0:T(8,128)S(1)}, f32[72,128]{1,0:T(8,128)S(1)}, f32[8,128]{1,0:T(8,128)S(1)}) custom-call(f32[3,1,128]{2,1,0:T(1,128)} %bitcast.1.positions_ref, s32[1,128]{1,0:T(1,128)} %bitcast.2.species_ref, s32[8,27]{1,0:T(8,128)} %bitcast.325, s32[1,2048]{1,0:T(1,128)} %bitcast.5.first_ref, ...), custom_call_target="tpu_custom_call" | custom-call | tf_op jit(solution)/shard_map/pallas_call | solution.py:1006
  2.5 2.7 %collective-permute-start.36 = (f32[72,128]{1,0:T(8,128)S(1)}, f32[72,128]{1,0:T(8,128)S(1)}, u32[]{:S(2)}, u32[]{:S(2)}) collective-permute-start(f32[72,128]{1,0:T(8,128)S(1)} %get-tuple-element.614.out_high_ref), channel_id=1, source_target_pairs={{0,32},{32,64},{64,96},{96,128},{128,160},{160,192},{192,224},{224... | collective-permute-start | bytes 110600 | tf_op jit(solution)/shard_map/ppermute | solution.py:909
  7.3 1.1 %fusion.151 = (bf16[256,32]{1,0:T(8,128)(2,1)S(1)}, bf16[256,32]{1,0:T(8,128)(2,1)S(1)}) fusion(bf16[136,256]{1,0:T(8,128)(2,1)} %param.33, bf16[25,64]{1,0:T(8,128)(2,1)S(1)} %mul.1362, bf16[25,64]{1,0:T(8,128)(2,1)S(1)} %add.367), kind=kOutput, calls=%fused_computation.451 | convolution fusion | flops 2215936 | bytes 104704 | tf_op jit(solution)/shard_map/dot_general | solution.py:330
  8.6 1.3 %collective-permute-start.38 = (f32[72,128]{1,0:T(8,128)S(1)}, f32[72,128]{1,0:T(8,128)S(1)}, u32[]{:S(2)}, u32[]{:S(2)}) collective-permute-start(f32[72,128]{1,0:T(8,128)S(1)} %pad_maximum_fusion.62), channel_id=1, source_target_pairs={{0,8},{8,16},{16,24},{24,0},{1,9},{9,17},{17,25},{25,1},{2,10},{10... | collective-permute-start | bytes 110600 | tf_op jit(solution)/shard_map/ppermute | solution.py:909
  9.9 1.5 %collective-permute-start.39 = (f32[72,128]{1,0:T(8,128)S(1)}, f32[72,128]{1,0:T(8,128)S(1)}, u32[]{:S(2)}, u32[]{:S(2)}) collective-permute-start(f32[72,128]{1,0:T(8,128)S(1)} %pad_maximum_fusion.63), channel_id=1, source_target_pairs={{0,24},{8,0},{16,8},{24,16},{1,25},{9,1},{17,9},{25,17},{2,26},{10... | collective-permute-start | bytes 110600 | tf_op jit(solution)/shard_map/ppermute | solution.py:909
  11.4 1.9 %shard_map.177.pairs_ref = f32[128,128]{1,0:T(8,128)S(1)} custom-call(f32[3,1,128]{2,1,0:T(1,128)} %bitcast.1.positions_ref, s32[1,128]{1,0:T(1,128)} %bitcast.2.species_ref, s32[1,2048]{1,0:T(1,128)} %bitcast.5.first_ref, s32[1,2048]{1,0:T(1,128)} %bitcast.6.second_ref), custom_call_target="tpu_custom_call" | custom-call | tf_op jit(solution)/shard_map/pallas_call | solution.py:932
  13.4 1.7 %collective-permute-start.40 = (f32[72,128]{1,0:T(8,128)S(1)}, f32[72,128]{1,0:T(8,128)S(1)}, u32[]{:S(2)}, u32[]{:S(2)}) collective-permute-start(f32[72,128]{1,0:T(8,128)S(1)} %get-tuple-element.621), channel_id=1, source_target_pairs={{0,1},{1,2},{2,3},{3,4},{4,5},{5,6},{6,7},{7,0},{8,9},{9,10},{10,1... | collective-permute-start | bytes 110600 | tf_op jit(solution)/shard_map/ppermute | solution.py:909
  15.1 4.0 %collective-permute-start.41 = (f32[72,128]{1,0:T(8,128)S(1)}, f32[72,128]{1,0:T(8,128)S(1)}, u32[]{:S(2)}, u32[]{:S(2)}) collective-permute-start(f32[72,128]{1,0:T(8,128)S(1)} %get-tuple-element.622), channel_id=1, source_target_pairs={{0,7},{1,0},{2,1},{3,2},{4,3},{5,4},{6,5},{7,6},{8,15},{9,8},{10,9... | collective-permute-start | bytes 110600 | tf_op jit(solution)/shard_map/ppermute | solution.py:909
  19.3 1.1 %collective-permute-done.40.in_low_ref = f32[72,128]{1,0:T(8,128)S(1)} collective-permute-done((f32[72,128]{1,0:T(8,128)S(1)}, f32[72,128]{1,0:T(8,128)S(1)}, u32[]{:S(2)}, u32[]{:S(2)}) %collective-permute-start.40) | collective-permute-done | bytes 36896 | tf_op jit(solution)/shard_map/ppermute | solution.py:909
  20.4 12.8 %shard_map.178 = (f32[16,128]{1,0:T(8,128)S(1)}, f32[80,128]{1,0:T(8,128)S(1)}, f32[72,128]{1,0:T(8,128)S(1)}, f32[80,128]{1,0:T(8,128)S(1)}, s32[54,128]{1,0:T(8,128)S(1)}, /*index=5*/f32[8,128]{1,0:T(8,128)S(1)}) custom-call(f32[72,128]{1,0:T(8,128)S(1)} %get-tuple-element.612.out_low_ref, f32[72,128]{1,0:T(8,128)S(1)} %get-tuple-element.613.out_mid_ref, ...), custom_call_target="tpu_custom_call" | custom-call | tf_op jit(solution)/shard_map/pallas_call | solution.py:1040
  33.2 6.6 %collective-permute-start.43 = (f32[80,128]{1,0:T(8,128)S(1)}, f32[80,128]{1,0:T(8,128)S(1)}, u32[]{:S(2)}, u32[]{:S(2)}) collective-permute-start(f32[80,128]{1,0:T(8,128)S(1)} %get-tuple-element.628), channel_id=1, source_target_pairs={{0,224},{32,0},{64,32},{96,64},{128,96},{160,128},{192,160},{224,1... | collective-permute-start | bytes 122888 | tf_op jit(solution)/shard_map/ppermute | solution.py:909
  39.8 1.7 %collective-permute-done.43 = f32[80,128]{1,0:T(8,128)S(1)} collective-permute-done((f32[80,128]{1,0:T(8,128)S(1)}, f32[80,128]{1,0:T(8,128)S(1)}, u32[]{:S(2)}, u32[]{:S(2)}) %collective-permute-start.43) | collective-permute-done | bytes 40992 | tf_op jit(solution)/shard_map/ppermute | solution.py:909
  41.5 2.0 %collective-permute-start.46 = (f32[8,128]{1,0:T(8,128)S(1)}, f32[8,128]{1,0:T(8,128)S(1)}, u32[]{:S(2)}, u32[]{:S(2)}) collective-permute-start(f32[8,128]{1,0:T(8,128)S(1)} %fusion.162), channel_id=1, source_target_pairs={{0,16},{8,24},{16,0},{24,8},{1,17},{9,25},{17,1},{25,9},{2,18},{10... | collective-permute-start | bytes 12296 | tf_op jit(solution)/shard_map/ppermute | solution.py:909
  43.5 1.4 %collective-permute-start.44 = (f32[80,128]{1,0:T(8,128)S(1)}, f32[80,128]{1,0:T(8,128)S(1)}, u32[]{:S(2)}, u32[]{:S(2)}) collective-permute-start(f32[80,128]{1,0:T(8,128)S(1)} %get-tuple-element.1293), channel_id=1, source_target_pairs={{0,8},{8,16},{16,24},{24,0},{1,9},{9,17},{17,25},{25,1},{2,10},{10... | collective-permute-start | bytes 122888 | tf_op jit(solution)/shard_map/ppermute | solution.py:909
  44.9 1.3 %collective-permute-start.45 = (f32[80,128]{1,0:T(8,128)S(1)}, f32[80,128]{1,0:T(8,128)S(1)}, u32[]{:S(2)}, u32[]{:S(2)}) collective-permute-start(f32[80,128]{1,0:T(8,128)S(1)} %get-tuple-element.1292), channel_id=1, source_target_pairs={{0,24},{8,0},{16,8},{24,16},{1,25},{9,1},{17,9},{25,17},{2,26},{10... | collective-permute-start | bytes 122888 | tf_op jit(solution)/shard_map/ppermute | solution.py:909
  46.2 1.4 %collective-permute-done.44 = f32[80,128]{1,0:T(8,128)S(1)} collective-permute-done((f32[80,128]{1,0:T(8,128)S(1)}, f32[80,128]{1,0:T(8,128)S(1)}, u32[]{:S(2)}, u32[]{:S(2)}) %collective-permute-start.44) | collective-permute-done | bytes 40992 | tf_op jit(solution)/shard_map/ppermute | solution.py:909
  48.1 2.7 %collective-permute-start.48 = (f32[80,128]{1,0:T(8,128)S(1)}, f32[80,128]{1,0:T(8,128)S(1)}, u32[]{:S(2)}, u32[]{:S(2)}) collective-permute-start(f32[80,128]{1,0:T(8,128)S(1)} %get-tuple-element.1122), channel_id=1, source_target_pairs={{0,7},{1,0},{2,1},{3,2},{4,3},{5,4},{6,5},{7,6},{8,15},{9,8},{10,9... | collective-permute-start | bytes 122888 | tf_op jit(solution)/shard_map/ppermute | solution.py:909
  50.8 1.3 %collective-permute-done.47.in_low_ref = f32[80,128]{1,0:T(8,128)S(1)} collective-permute-done((f32[80,128]{1,0:T(8,128)S(1)}, f32[80,128]{1,0:T(8,128)S(1)}, u32[]{:S(2)}, u32[]{:S(2)}) %collective-permute-start.47) | collective-permute-done | bytes 40992 | tf_op jit(solution)/shard_map/ppermute | solution.py:909
  52.2 3.4 %collective-permute-start.49 = (f32[8,128]{1,0:T(8,128)S(1)}, f32[8,128]{1,0:T(8,128)S(1)}, u32[]{:S(2)}, u32[]{:S(2)}) collective-permute-start(f32[8,128]{1,0:T(8,128)S(1)} %fusion.161), channel_id=1, source_target_pairs={{0,128},{32,160},{64,192},{96,224},{128,0},{160,32},{192,64},{224,... | collective-permute-start | bytes 12296 | tf_op jit(solution)/shard_map/ppermute | solution.py:909
  55.5 1.0 %collective-permute-done.49 = f32[8,128]{1,0:T(8,128)S(1)} collective-permute-done((f32[8,128]{1,0:T(8,128)S(1)}, f32[8,128]{1,0:T(8,128)S(1)}, u32[]{:S(2)}, u32[]{:S(2)}) %collective-permute-start.49) | collective-permute-done | bytes 4128 | tf_op jit(solution)/shard_map/ppermute | solution.py:909
  56.5 6.6 %collective-permute-start.50 = (f32[8,128]{1,0:T(8,128)S(1)}, f32[8,128]{1,0:T(8,128)S(1)}, u32[]{:S(2)}, u32[]{:S(2)}) collective-permute-start(f32[8,128]{1,0:T(8,128)S(1)} %add.376), channel_id=1, source_target_pairs={{0,32},{32,0},{64,96},{96,64},{128,160},{160,128},{192,224},{224,1... | collective-permute-start | bytes 12296 | tf_op jit(solution)/shard_map/ppermute | solution.py:982
  64.0 4.1 %collective-permute-start.51 = (f32[1,128]{1,0:T(1,128)S(1)}, f32[1,128]{1,0:T(1,128)S(1)}, u32[]{:S(2)}, u32[]{:S(2)}) collective-permute-start(f32[1,128]{1,0:T(1,128)S(1)} %broadcast_select_fusion), channel_id=1, source_target_pairs={{0,5},{1,6},{2,7},{3,0},{4,1},{5,2},{6,3},{7,4},{32,35},{33,36},{3... | collective-permute-start | bytes 1544 | tf_op jit(solution)/shard_map/ppermute | solution.py:977
  68.0 1.4 %collective-permute-done.51 = f32[1,128]{1,0:T(1,128)S(1)} collective-permute-done((f32[1,128]{1,0:T(1,128)S(1)}, f32[1,128]{1,0:T(1,128)S(1)}, u32[]{:S(2)}, u32[]{:S(2)}) %collective-permute-start.51) | collective-permute-done | bytes 544 | tf_op jit(solution)/shard_map/ppermute | solution.py:977
  70.2 1.1 %shard_map.179 = f32[3,1,128]{2,1,0:T(1,128)} custom-call(f32[16,128]{1,0:T(8,128)S(1)} %get-tuple-element.625.own_ref, f32[80,128]{1,0:T(8,128)S(1)} %collective-permute-done.47.in_low_ref, f32[72,128]{1,0:T(8,128)S(1)} %get-tuple-element.1226.in_mid_ref, f32[80,128]{1,0:T(8,128)S(1)} %collective-permute-done.48.in_high_ref, ...), custom_call_target="tpu_custom_call" | custom-call | tf_op jit(solution)/shard_map/pallas_call | solution.py:1088
  (70 shorter events, 5.5 us)
Async XLA Ops:
  0.6 72.7 %copy-start.54 = (s32[1,1,1,27,8]{3,4,2,1,0:T(8,128)S(1)}, s32[1,1,1,27,8]{3,4,2,1,0:T(8,128)}, u32[]{:S(2)}) copy-start(s32[1,1,1,27,8]{3,4,2,1,0:T(8,128)} %param.29) | copy-start | bytes 2596
  0.6 72.7 %copy-start.31 = (bf16[136,256]{1,0:T(8,128)(2,1)S(1)}, bf16[136,256]{1,0:T(8,128)(2,1)}, u32[]{:S(2)}) copy-start(bf16[136,256]{1,0:T(8,128)(2,1)} %param.33) | copy-start | bytes 208900
  0.7 72.7 %copy-start.23 = (f32[5,64]{1,0:T(8,128)S(1)}, f32[5,64]{1,0:T(8,128)}, u32[]{:S(2)}) copy-start(f32[5,64]{1,0:T(8,128)} %param.32) | copy-start | bytes 3844
  0.7 72.7 %copy-start.12 = (bf16[256,192]{0,1:T(8,128)(2,1)S(1)}, bf16[256,192]{0,1:T(8,128)(2,1)}, u32[]{:S(2)}) copy-start(bf16[256,192]{0,1:T(8,128)(2,1)} %param.34) | copy-start | bytes 294916
  0.7 72.7 %copy-start.20 = (bf16[192,128]{1,0:T(8,128)(2,1)S(1)}, bf16[192,128]{1,0:T(8,128)(2,1)}, u32[]{:S(2)}) copy-start(bf16[192,128]{1,0:T(8,128)(2,1)} %inv_w_ref.1) | copy-start | bytes 147460
  2.5 6.0 %collective-permute-start.36 = (f32[72,128]{1,0:T(8,128)S(1)}, f32[72,128]{1,0:T(8,128)S(1)}, u32[]{:S(2)}, u32[]{:S(2)}) collective-permute-start(f32[72,128]{1,0:T(8,128)S(1)} %get-tuple-element.614.out_high_ref), channel_id=1, source_target_pairs={{0,32},{32,64},{64,96},{96,128},{128,160},{160,192},{192,224},{224... | collective-permute-start | bytes 110600 | tf_op jit(solution)/shard_map/ppermute | solution.py:909
  5.2 3.4 %collective-permute-start.37 = (f32[72,128]{1,0:T(8,128)S(1)}, f32[72,128]{1,0:T(8,128)S(1)}, u32[]{:S(2)}, u32[]{:S(2)}) collective-permute-start(f32[72,128]{1,0:T(8,128)S(1)} %get-tuple-element.612.out_low_ref), channel_id=1, source_target_pairs={{0,224},{32,0},{64,32},{96,64},{128,96},{160,128},{192,160},{224,1... | collective-permute-start | bytes 110600 | tf_op jit(solution)/shard_map/ppermute | solution.py:909
  8.6 4.7 %collective-permute-start.38 = (f32[72,128]{1,0:T(8,128)S(1)}, f32[72,128]{1,0:T(8,128)S(1)}, u32[]{:S(2)}, u32[]{:S(2)}) collective-permute-start(f32[72,128]{1,0:T(8,128)S(1)} %pad_maximum_fusion.62), channel_id=1, source_target_pairs={{0,8},{8,16},{16,24},{24,0},{1,9},{9,17},{17,25},{25,1},{2,10},{10... | collective-permute-start | bytes 110600 | tf_op jit(solution)/shard_map/ppermute | solution.py:909
  9.9 3.4 %collective-permute-start.39 = (f32[72,128]{1,0:T(8,128)S(1)}, f32[72,128]{1,0:T(8,128)S(1)}, u32[]{:S(2)}, u32[]{:S(2)}) collective-permute-start(f32[72,128]{1,0:T(8,128)S(1)} %pad_maximum_fusion.63), channel_id=1, source_target_pairs={{0,24},{8,0},{16,8},{24,16},{1,25},{9,1},{17,9},{25,17},{2,26},{10... | collective-permute-start | bytes 110600 | tf_op jit(solution)/shard_map/ppermute | solution.py:909
  13.4 7.0 %collective-permute-start.40 = (f32[72,128]{1,0:T(8,128)S(1)}, f32[72,128]{1,0:T(8,128)S(1)}, u32[]{:S(2)}, u32[]{:S(2)}) collective-permute-start(f32[72,128]{1,0:T(8,128)S(1)} %get-tuple-element.621), channel_id=1, source_target_pairs={{0,1},{1,2},{2,3},{3,4},{4,5},{5,6},{6,7},{7,0},{8,9},{9,10},{10,1... | collective-permute-start | bytes 110600 | tf_op jit(solution)/shard_map/ppermute | solution.py:909
  15.1 5.3 %collective-permute-start.41 = (f32[72,128]{1,0:T(8,128)S(1)}, f32[72,128]{1,0:T(8,128)S(1)}, u32[]{:S(2)}, u32[]{:S(2)}) collective-permute-start(f32[72,128]{1,0:T(8,128)S(1)} %get-tuple-element.622), channel_id=1, source_target_pairs={{0,7},{1,0},{2,1},{3,2},{4,3},{5,4},{6,5},{7,6},{8,15},{9,8},{10,9... | collective-permute-start | bytes 110600 | tf_op jit(solution)/shard_map/ppermute | solution.py:909
  33.2 8.3 %collective-permute-start.43 = (f32[80,128]{1,0:T(8,128)S(1)}, f32[80,128]{1,0:T(8,128)S(1)}, u32[]{:S(2)}, u32[]{:S(2)}) collective-permute-start(f32[80,128]{1,0:T(8,128)S(1)} %get-tuple-element.628), channel_id=1, source_target_pairs={{0,224},{32,0},{64,32},{96,64},{128,96},{160,128},{192,160},{224,1... | collective-permute-start | bytes 122888 | tf_op jit(solution)/shard_map/ppermute | solution.py:909
  39.8 1.7 %collective-permute-start.42 = (f32[80,128]{1,0:T(8,128)S(1)}, f32[80,128]{1,0:T(8,128)S(1)}, u32[]{:S(2)}, u32[]{:S(2)}) collective-permute-start(f32[80,128]{1,0:T(8,128)S(1)} %get-tuple-element.626), channel_id=1, source_target_pairs={{0,32},{32,64},{64,96},{96,128},{128,160},{160,192},{192,224},{224... | collective-permute-start | bytes 122888 | tf_op jit(solution)/shard_map/ppermute | solution.py:909
  41.5 4.8 %collective-permute-start.46 = (f32[8,128]{1,0:T(8,128)S(1)}, f32[8,128]{1,0:T(8,128)S(1)}, u32[]{:S(2)}, u32[]{:S(2)}) collective-permute-start(f32[8,128]{1,0:T(8,128)S(1)} %fusion.162), channel_id=1, source_target_pairs={{0,16},{8,24},{16,0},{24,8},{1,17},{9,25},{17,1},{25,9},{2,18},{10... | collective-permute-start | bytes 12296 | tf_op jit(solution)/shard_map/ppermute | solution.py:909
  43.5 4.1 %collective-permute-start.44 = (f32[80,128]{1,0:T(8,128)S(1)}, f32[80,128]{1,0:T(8,128)S(1)}, u32[]{:S(2)}, u32[]{:S(2)}) collective-permute-start(f32[80,128]{1,0:T(8,128)S(1)} %get-tuple-element.1293), channel_id=1, source_target_pairs={{0,8},{8,16},{16,24},{24,0},{1,9},{9,17},{17,25},{25,1},{2,10},{10... | collective-permute-start | bytes 122888 | tf_op jit(solution)/shard_map/ppermute | solution.py:909
  44.9 2.9 %collective-permute-start.45 = (f32[80,128]{1,0:T(8,128)S(1)}, f32[80,128]{1,0:T(8,128)S(1)}, u32[]{:S(2)}, u32[]{:S(2)}) collective-permute-start(f32[80,128]{1,0:T(8,128)S(1)} %get-tuple-element.1292), channel_id=1, source_target_pairs={{0,24},{8,0},{16,8},{24,16},{1,25},{9,1},{17,9},{25,17},{2,26},{10... | collective-permute-start | bytes 122888 | tf_op jit(solution)/shard_map/ppermute | solution.py:909
  47.9 4.2 %collective-permute-start.47 = (f32[80,128]{1,0:T(8,128)S(1)}, f32[80,128]{1,0:T(8,128)S(1)}, u32[]{:S(2)}, u32[]{:S(2)}) collective-permute-start(f32[80,128]{1,0:T(8,128)S(1)} %constant_dynamic-update-slice_fusion.27), channel_id=1, source_target_pairs={{0,1},{1,2},{2,3},{3,4},{4,5},{5,6},{6,7},{7,0},{8,9},{9,10},{10,1... | collective-permute-start | bytes 122888 | tf_op jit(solution)/shard_map/ppermute | solution.py:909
  48.1 4.0 %collective-permute-start.48 = (f32[80,128]{1,0:T(8,128)S(1)}, f32[80,128]{1,0:T(8,128)S(1)}, u32[]{:S(2)}, u32[]{:S(2)}) collective-permute-start(f32[80,128]{1,0:T(8,128)S(1)} %get-tuple-element.1122), channel_id=1, source_target_pairs={{0,7},{1,0},{2,1},{3,2},{4,3},{5,4},{6,5},{7,6},{8,15},{9,8},{10,9... | collective-permute-start | bytes 122888 | tf_op jit(solution)/shard_map/ppermute | solution.py:909
  52.2 4.4 %collective-permute-start.49 = (f32[8,128]{1,0:T(8,128)S(1)}, f32[8,128]{1,0:T(8,128)S(1)}, u32[]{:S(2)}, u32[]{:S(2)}) collective-permute-start(f32[8,128]{1,0:T(8,128)S(1)} %fusion.161), channel_id=1, source_target_pairs={{0,128},{32,160},{64,192},{96,224},{128,0},{160,32},{192,64},{224,... | collective-permute-start | bytes 12296 | tf_op jit(solution)/shard_map/ppermute | solution.py:909
  56.5 7.4 %collective-permute-start.50 = (f32[8,128]{1,0:T(8,128)S(1)}, f32[8,128]{1,0:T(8,128)S(1)}, u32[]{:S(2)}, u32[]{:S(2)}) collective-permute-start(f32[8,128]{1,0:T(8,128)S(1)} %add.376), channel_id=1, source_target_pairs={{0,32},{32,0},{64,96},{96,64},{128,160},{160,128},{192,224},{224,1... | collective-permute-start | bytes 12296 | tf_op jit(solution)/shard_map/ppermute | solution.py:982
  64.0 5.4 %collective-permute-start.51 = (f32[1,128]{1,0:T(1,128)S(1)}, f32[1,128]{1,0:T(1,128)S(1)}, u32[]{:S(2)}, u32[]{:S(2)}) collective-permute-start(f32[1,128]{1,0:T(1,128)S(1)} %broadcast_select_fusion), channel_id=1, source_target_pairs={{0,5},{1,6},{2,7},{3,0},{4,1},{5,2},{6,3},{7,4},{32,35},{33,36},{3... | collective-permute-start | bytes 1544 | tf_op jit(solution)/shard_map/ppermute | solution.py:977
  69.4 2.0 %collective-permute-start.52 = (f32[1,128]{1,0:T(1,128)S(1)}, f32[1,128]{1,0:T(1,128)S(1)}, u32[]{:S(2)}, u32[]{:S(2)}) collective-permute-start(f32[1,128]{1,0:T(1,128)S(1)} %collective-permute-done.51), channel_id=1, source_target_pairs={{0,32},{32,0},{64,96},{96,64},{128,160},{160,128},{192,224},{224,1... | collective-permute-start | bytes 1544 | tf_op jit(solution)/shard_map/ppermute | solution.py:982
